TPU v7x, 512 devices: a whole 4x4x16 slice. The times are simulated.
512 devices in a mesh: group: 8 (over y, core), dev: 64 (over x, z).
Axes of the slice: x: 4, y: 4, z: 16, core: 2. Of those that a mesh axis runs over, the one named last changes fastest.
Arguments:
- bin_index: int32 [2097152, 128], P(('group', 'dev')), may hold values from 0 to 63
- gradient: bfloat16 [2097152], P(('group', 'dev')), may hold values from -6 to 6
- hessian: bfloat16 [2097152], P(('group', 'dev')), may hold values from 0.049804688 to 0.25
- child_id: int32 [2097152], P(('group', 'dev')), may hold values from 0 to 63
- smaller_side: int32 [32], replicated, may hold values from 0 to 1
Outputs:
- best_gain: float32 [32, 128], P('group', 'dev')
- child_best: float32 [32], P('group')
All inputs are finite; a program needn't handle non-finite values.
Results may differ from a plain program's by a relative error of at most 0.0003.
Values sent between devices are 32-bit elements; how exact they have to be, the bound alone decides.
No kernel may reach another device: no remote copies, remote signals or barrier semaphores. Data moves between devices by JAX's collectives and lax.ppermute only.
A program may use at most 64 MiB of HBM per device.

v0:
```python
import functools
import math

import jax
import jax.numpy as jnp
from jax import lax
from jax.sharding import Mesh
from jax.sharding import PartitionSpec as P

BINS = 64
DEV = ("dev_0", "dev_1")
GROUP_DEV = ("group", "dev_0", "dev_1")


reg_lambda = 1.0


def cut_along(array, dim, count):
    before, after = (array.shape[:dim], array.shape[dim + 1 :])
    return jnp.moveaxis(array.reshape(*before, count, -1, *after), dim, 0)


def sum_at_owner(array, axis, dim):
    count = lax.axis_size(axis)
    pieces = lax.all_to_all(cut_along(array, dim, count), axis, 0, 0, tiled=True)
    return jnp.sum(pieces, axis=0)


def summed_rows(array, axes, dim):
    far, near = axes
    return sum_at_owner(sum_at_owner(array, far, dim), near, dim)


def by_axis(array, axes):
    return functools.reduce(lax.pmax, axes, array)


def split_gains(hist_grad, hist_hess):
    left_grad = jnp.cumsum(hist_grad, axis=-1)[..., :-1]
    left_hess = jnp.cumsum(hist_hess, axis=-1)[..., :-1]
    total_grad = jnp.sum(hist_grad, axis=-1, keepdims=True)
    total_hess = jnp.sum(hist_hess, axis=-1, keepdims=True)
    right_grad = total_grad - left_grad
    value = left_grad * left_grad / (left_hess + reg_lambda)
    value = value + right_grad * right_grad / (total_hess - left_hess + reg_lambda)
    value = value - total_grad * total_grad / (total_hess + reg_lambda)
    return jnp.max(value, axis=-1)


def build_block(bin_index, weights, count):
    block_size = math.gcd(count, 8)
    leaves = weights.shape[1] // 2
    levels = jnp.arange(BINS, dtype=jnp.int32)

    def one_block(number):
        columns = lax.dynamic_slice_in_dim(bin_index, number * block_size, block_size, 1)
        onehot = (columns[:, :, None] == levels[None, None, :]).astype(jnp.bfloat16)
        onehot = onehot.reshape(columns.shape[0], block_size * BINS)
        product = lax.dot_general(
            onehot, weights, (((0,), (0,)), ((), ())), preferred_element_type=jnp.float32
        )
        product = product.reshape(block_size, BINS, 2, leaves).transpose(0, 3, 2, 1)
        return product.reshape(block_size, leaves, 2 * BINS)

    stacked = lax.map(one_block, jnp.arange(count // block_size, dtype=jnp.int32))
    return stacked.reshape(count, leaves, 2 * BINS)


def body(bin_index, gradient, hessian, child_id, smaller_side):
    leaves = smaller_side.shape[0]
    features = bin_index.shape[1]
    target = 2 * jnp.arange(leaves, dtype=jnp.int32)[None, :] + smaller_side[None, :]
    chosen = child_id[:, None] == target
    nothing = jnp.zeros((), jnp.bfloat16)
    weights = jnp.concatenate(
        [
            jnp.where(chosen, gradient[:, None], nothing),
            jnp.where(chosen, hessian[:, None], nothing),
        ],
        axis=1,
    )
    local_rows = features // lax.axis_size(DEV)
    owned = summed_rows(
        build_block(bin_index, weights, local_rows * lax.axis_size(DEV)), ("dev_0", "dev_1"), 0
    )
    owned = sum_at_owner(owned, "group", 1)
    hist_grad = owned[:, :, :BINS].transpose(1, 0, 2)
    hist_hess = owned[:, :, BINS:].transpose(1, 0, 2)
    best_gain = split_gains(hist_grad, hist_hess)
    child_best = by_axis(jnp.max(best_gain, axis=1), DEV)
    return (best_gain, child_best)


def solution(mesh):
    split = Mesh(mesh.devices.reshape(mesh.shape["group"], 4, 16), ("group", "dev_0", "dev_1"))
    return jax.shard_map(
        body,
        mesh=split,
        in_specs=(P(GROUP_DEV, None), P(GROUP_DEV), P(GROUP_DEV), P(GROUP_DEV), P()),
        out_specs=(P("group", DEV), P("group")),
        check_vma=False,
    )
```

profile of v0, /device:TPU:2, one launch (start us, length us, event | category | flops | bytes accessed | tf_op | source)
XLA Modules:
  0.0 224.3 jit_solution(12308217171837098945)
XLA Ops:
  0.6 0.7 multiply_add_fusion
  1.3 2.0 copy.33
  3.5 93.9 %while.11 = (s32[]{:T(128)}, f32[16,8,32,128]{3,2,1,0:T(8,128)}, s32[16]{0:T(128)S(1)}, s32[4096,128]{0,1:T(8,128)S(1)}, bf16[4096,64]{0,1:T(8,128)(2,1)S(1)}, /...) while((s32[]{:T(128)}, f32[16,8,32,128]{3,2,1,0:T(8,128)}, s32[16]{0:T(128)S(1)}, ...), condition=%wide.region_1.2_spmd.clone, body=%wide.region_0.1_spmd.clone.sunk | while | flops 270532608 | bytes 6038171 | solution.py:65
  3.5 0.6 dynamic_slice.13
  4.9 1.3 bitcast_compare_fusion.2
  6.2 2.1 convolution_bitcast_fusion.2
  8.7 0.6 constant_dynamic-update-slice_fusion.2
  10.7 1.3 bitcast_compare_fusion.2
  12.1 2.1 convolution_bitcast_fusion.2
  14.6 0.7 constant_dynamic-update-slice_fusion.2
  16.6 1.3 bitcast_compare_fusion.2
  17.9 2.1 convolution_bitcast_fusion.2
  20.5 0.7 constant_dynamic-update-slice_fusion.2
  21.1 0.6 dynamic_slice.13
  22.5 1.3 bitcast_compare_fusion.2
  23.8 2.1 convolution_bitcast_fusion.2
  26.3 0.7 constant_dynamic-update-slice_fusion.2
  27.0 0.6 dynamic_slice.13
  28.3 1.3 bitcast_compare_fusion.2
  29.7 2.1 convolution_bitcast_fusion.2
  32.2 0.7 constant_dynamic-update-slice_fusion.2
  32.9 0.6 dynamic_slice.13
  34.2 1.3 bitcast_compare_fusion.2
  35.5 2.1 convolution_bitcast_fusion.2
  38.1 0.6 constant_dynamic-update-slice_fusion.2
  38.7 0.6 dynamic_slice.13
  40.1 1.3 bitcast_compare_fusion.2
  41.4 2.1 convolution_bitcast_fusion.2
  43.9 0.7 constant_dynamic-update-slice_fusion.2
  45.9 1.3 bitcast_compare_fusion.2
  47.3 2.1 convolution_bitcast_fusion.2
  49.8 0.7 constant_dynamic-update-slice_fusion.2
  51.8 1.3 bitcast_compare_fusion.2
  53.2 2.1 convolution_bitcast_fusion.2
  55.7 0.7 constant_dynamic-update-slice_fusion.2
  57.7 1.3 bitcast_compare_fusion.2
  59.0 2.1 convolution_bitcast_fusion.2
  61.6 0.7 constant_dynamic-update-slice_fusion.2
  63.6 1.3 bitcast_compare_fusion.2
  64.9 2.1 convolution_bitcast_fusion.2
  67.4 0.7 constant_dynamic-update-slice_fusion.2
  69.4 1.3 bitcast_compare_fusion.2
  70.8 2.1 convolution_bitcast_fusion.2
  73.3 0.7 constant_dynamic-update-slice_fusion.2
  75.3 1.3 bitcast_compare_fusion.2
  76.6 2.1 convolution_bitcast_fusion.2
  79.2 0.7 constant_dynamic-update-slice_fusion.2
  81.2 1.3 bitcast_compare_fusion.2
  82.5 2.1 convolution_bitcast_fusion.2
  85.0 0.7 constant_dynamic-update-slice_fusion.2
  87.0 1.3 bitcast_compare_fusion.2
  88.4 2.1 convolution_bitcast_fusion.2
  90.9 0.7 constant_dynamic-update-slice_fusion.2
  92.9 1.3 bitcast_compare_fusion.2
  94.2 2.1 convolution_bitcast_fusion.2
  96.8 0.7 constant_dynamic-update-slice_fusion.2
  97.4 29.7 %all_to_all.15 = f32[4,32,32,128]{3,2,1,0:T(8,128)S(1)} all-to-all(f32[4,32,32,128]{3,2,1,0:T(8,128)} %bitcast.47), channel_id=1, replica_groups=mesh['group'=8,'dev_0'=4,'dev_1'=16] {'dev_0'}, dimensions={0} | all-to-all | bytes 4194304 | tf_op jit(solution)/shard_map/all_to_all | solution.py:25
  127.4 42.4 %all_to_all.16 = f32[16,2,32,128]{3,2,1,0:T(8,128)S(1)} all-to-all(f32[16,2,32,128]{3,2,1,0:T(8,128)S(1)} %bitcast.48), channel_id=1, replica_groups=mesh['group'=8,'dev_0'=4,'dev_1'=16] {'dev_1'}, dimensions={0} | all-to-all | bytes 1048576 | tf_op jit(solution)/shard_map/all_to_all | solution.py:25
  169.8 9.7 %all_to_all.17 = f32[8,2,4,128]{3,2,1,0:T(4,128)S(1)} all-to-all(f32[8,2,4,128]{3,2,1,0:T(4,128)S(1)} %copy.34), channel_id=1, replica_groups=mesh['group'=8,'dev_0'=4,'dev_1'=16] {'group'}, dimensions={0} | all-to-all | bytes 65536 | tf_op jit(solution)/shard_map/all_to_all | solution.py:25
  180.0 0.9 reduce_window_sum.17
  181.0 0.9 reduce_window_sum.18
  182.1 9.2 %pmax.14 = f32[4]{0:T(128)S(1)} all-reduce(f32[4]{0:T(128)S(1)} %get-tuple-element.92), channel_id=1, replica_groups=mesh['group'=8,'dev_0'=4,'dev_1'=16] {'dev_0'}, use_global_device_ids=true, to_apply=%region_11.12 | all-reduce | flops 4 | bytes 32 | tf_op jit(solution)/shard_map/pmax | solution.py:35
  191.3 0.6 copy.40
  192.0 32.4 %pmax.15 = f32[4]{0:T(128)} all-reduce(f32[4]{0:T(128)S(1)} %pmax.14), channel_id=1, replica_groups=mesh['group'=8,'dev_0'=4,'dev_1'=16] {'dev_1'}, use_global_device_ids=true, to_apply=%region_12.13 | all-reduce | flops 4 | bytes 32 | tf_op jit(solution)/shard_map/pmax | solution.py:35
  (114 shorter events, 15.4 us)
Async XLA Ops:
  1.3 2.0 copy-start
  1.3 2.0 copy-start.1
  1.3 2.0 copy-start.2
where the time goes:
time: 225 us; the launch traced here: 224 us
  blocking collectives  123 us (55%)
  matrix products  34.1 us (15%)
  local copies, waits for them, and re-layouts  30.7 us (14%)
  other arithmetic  24.5 us (11%)
  loops' own time  11 us (5%)
    all_to_all x3, blocking collectives, sum_at_owner(): lax.all_to_all(cut_along(array, dim, count), axis, 0, 0, tiled=True)  81.8 us
    pmax x2, blocking collectives, by_axis(): return functools.reduce(lax.pmax, axes, array)  41.6 us
    dot_general x16, matrix products, one_block(): lax.dot_general(onehot, weights, (((0,), (0,)), ((), ())), preferred_elem...  34.1 us
    eq x16, other arithmetic, one_block(): onehot = (columns[:, :, None] == levels[None, None, :]).astype(jnp.bfloat16)  21.1 us
    another operation x1, loops' own time, build_block(): lax.map(one_block, jnp.arange(count // block_size, dtype=jnp.int32))  11 us
    dynamic_update_slice x16, local copies, waits for them, and re-layouts, build_block(): lax.map(one_block, jnp.arange(count // block_size, dtype=jnp.int32))  10.5 us
    dynamic_slice x16, local copies, waits for them, and re-layouts, build_block(): lax.map(one_block, jnp.arange(count // block_size, dtype=jnp.int32))  9.32 us

commit v1 on v0

v1 whole, which is shorter than its diff:
```python
import functools

import jax
import jax.numpy as jnp
from jax import lax
from jax.experimental import pallas as pl
from jax.experimental.pallas import tpu as pltpu
from jax.sharding import Mesh
from jax.sharding import PartitionSpec as P

BINS = 64
LANES = 128
AXES = ("y", "core", "x", "z")
reg_lambda = 1.0


def hist_kernel(block, together, bin_ref, grad_ref, hess_ref, child_ref, target_ref,
                keep_ref, send_ref, turned, weights):
    rows, features = bin_ref.shape
    blocks = rows // block
    wide = block // LANES
    columns = target_ref.shape[0]
    is_grad = lax.broadcasted_iota(jnp.int32, (8, block), 0) < 4
    for k in range(blocks):
        turned[k] = bin_ref[k * block : (k + 1) * block, :].astype(jnp.float32).T
        parts = range(k * wide, (k + 1) * wide)
        child = jnp.concatenate([child_ref[i : i + 1, :] for i in parts], axis=1)
        grad = jnp.concatenate([grad_ref[i : i + 1, :] for i in parts], axis=1)
        hess = jnp.concatenate([hess_ref[i : i + 1, :] for i in parts], axis=1)
        value = jnp.where(is_grad, grad, hess)
        chosen = [
            child == jnp.concatenate([target_ref[8 * n : 8 * n + 8, :]] * wide, axis=1)
            for n in range(columns // 8)
        ]
        weights[k] = jnp.concatenate(
            [jnp.where(c, value, 0.0) for c in chosen], axis=0
        ).astype(jnp.bfloat16)

    level = lax.broadcasted_iota(jnp.int32, (16, block), 0).astype(jnp.float32)
    levels = [(level + 16.0 * n).astype(jnp.bfloat16) for n in range(BINS // 16)]
    one = jnp.ones((16, block), jnp.bfloat16)
    zero = jnp.zeros((16, block), jnp.bfloat16)

    def some_features(group, carry):
        total = jnp.zeros((columns, together * BINS), jnp.float32)
        for k in range(blocks):
            upto = []
            for i in range(together):
                row = turned[k, pl.ds(group * together + i, 1), :]
                row = jnp.broadcast_to(row, (16, block)).astype(jnp.bfloat16)
                upto += [jnp.where(row <= level, one, zero) for level in levels]
            total = total + lax.dot_general(
                weights[k], jnp.concatenate(upto, axis=0), (((1,), (1,)), ((), ())),
                preferred_element_type=jnp.float32,
            )
        for pair in range(together * BINS // LANES):
            owner = group * (together * BINS // LANES) + pair
            for n in range(columns // 8):
                piece = total[8 * n : 8 * n + 8, pair * LANES : (pair + 1) * LANES]
                out = keep_ref if n < columns // 16 else send_ref
                out[n % (columns // 16), owner] = piece
        return carry

    lax.fori_loop(0, features // together, some_features, 0)


def histograms(bin_index, gradient, hessian, child_id, target, block=512, together=8):
    rows, features = bin_index.shape
    columns = target.shape[0]
    half = jax.ShapeDtypeStruct((columns // 16, features * BINS // LANES, 8, LANES), jnp.float32)
    vmem = pl.BlockSpec(memory_space=pltpu.VMEM)
    return pl.pallas_call(
        functools.partial(hist_kernel, block, together),
        out_shape=(half, half),
        in_specs=[vmem] * 5,
        out_specs=(vmem, vmem),
        scratch_shapes=[
            pltpu.VMEM((rows // block, features, block), jnp.float32),
            pltpu.VMEM((rows // block, columns, block), jnp.bfloat16),
        ],
        compiler_params=pltpu.CompilerParams(vmem_limit_bytes=48 * 2**20),
        name="histograms",
    )(bin_index, gradient, hessian, child_id, target)


def gain_kernel(pieces_ref, best_ref, told_ref):
    left = jnp.sum(pieces_ref[...], axis=0)
    lane = lax.broadcasted_iota(jnp.int32, (8, LANES), 1)
    first = jnp.sum(jnp.where(lane == BINS - 1, left, 0.0), axis=1, keepdims=True)
    second = jnp.sum(jnp.where(lane == 2 * BINS - 1, left, 0.0), axis=1, keepdims=True)
    total = jnp.where(lane < BINS, first, second)
    left_grad, left_hess = left[:4], left[4:]
    total_grad, total_hess = total[:4], total[4:]
    right_grad = total_grad - left_grad
    value = left_grad * left_grad / (left_hess + reg_lambda)
    value = value + right_grad * right_grad / (total_hess - left_hess + reg_lambda)
    value = value - total_grad * total_grad / (total_hess + reg_lambda)
    lane = lane[:4]
    bottom = jnp.float32(-jnp.inf)
    inner = lane % BINS < BINS - 1
    one = jnp.max(jnp.where(inner & (lane < BINS), value, bottom), axis=1, keepdims=True)
    two = jnp.max(jnp.where(inner & (lane >= BINS), value, bottom), axis=1, keepdims=True)
    best_ref[...] = jnp.concatenate([one, two], axis=1)
    diagonal = lane == lax.broadcasted_iota(jnp.int32, (4, LANES), 0)
    told = jnp.sum(jnp.where(diagonal, jnp.maximum(one, two), 0.0), axis=0, keepdims=True)
    told_ref[...] = jnp.broadcast_to(told, told_ref.shape)


def gains(pieces, listeners):
    vmem = pl.BlockSpec(memory_space=pltpu.VMEM)
    return pl.pallas_call(
        gain_kernel,
        out_shape=(
            jax.ShapeDtypeStruct((4, 2), jnp.float32),
            jax.ShapeDtypeStruct((listeners, LANES), jnp.float32),
        ),
        in_specs=[vmem],
        out_specs=(vmem, vmem),
        name="gains",
    )(pieces)


def body(bin_index, gradient, hessian, child_id, smaller_side):
    ny, nc, nx, nz = (lax.axis_size(a) for a in AXES)
    rows = bin_index.shape[0]
    mine = lax.axis_index("core")
    leaves = 2 * jnp.arange(smaller_side.shape[0], dtype=jnp.int32) + smaller_side
    leaves = leaves.reshape(ny, nc, 4)
    ordered = jnp.stack(
        [
            jnp.where(mine == 0, leaves[:, 0], leaves[:, 1]),
            jnp.where(mine == 0, leaves[:, 1], leaves[:, 0]),
        ]
    )
    target = jnp.broadcast_to(ordered[:, :, None, :, None], (nc, ny, 2, 4, LANES))
    target = target.reshape(-1, LANES)
    keep, send = histograms(
        bin_index,
        gradient.astype(jnp.float32).reshape(rows // LANES, LANES),
        hessian.astype(jnp.float32).reshape(rows // LANES, LANES),
        child_id.reshape(rows // LANES, LANES),
        target,
    )
    chip = keep + lax.ppermute(send, "core", [(0, 1), (1, 0)])
    chip = chip.reshape(ny * nx, nz, 8, LANES)
    plane = jnp.sum(lax.all_to_all(chip, ("y", "x"), 0, 0, tiled=True), axis=0)
    pieces = lax.all_to_all(plane, "z", 0, 0, tiled=True)
    best_gain, told = gains(pieces, nx * nz)
    heard = lax.all_to_all(told, ("x", "z"), 0, 0, tiled=True)
    child_best = jnp.max(heard, axis=0)[:4]
    return best_gain, child_best


def solution(mesh):
    split = Mesh(mesh.devices.reshape(4, 2, 4, 16), AXES)
    every = P(AXES)
    return jax.shard_map(
        body,
        mesh=split,
        in_specs=(P(AXES, None), every, every, every, P()),
        out_specs=(P(("y", "core"), ("x", "z")), P(("y", "core"))),
        check_vma=False,
    )
```

time: 225 us -> 105 us (0.47)
  blocking collectives: 123 us -> 51.3 us
  matrix products: 34.1 us -> 0 us
  local copies, waits for them, and re-layouts: 30.7 us -> 3.86 us
  Pallas kernels: 0 us -> 24.6 us
  other arithmetic: 24.5 us -> 2.15 us
  waiting for transfers between devices: 0 us -> 14.7 us
  loops' own time: 11 us -> 0 us
  starting transfers between devices: 0 us -> 7.45 us
    pmax x2 -> x0, blocking collectives: 41.6 us -> none  [by_axis(): return functools.reduce(lax.pmax, axes, array)]
    dot_general x16 -> x0, matrix products: 34.1 us -> none  [one_block(): lax.dot_general(onehot, weights, (((0,), (0,)), ((), ())), preferred_elem...]
    all_to_all x3 -> x2, blocking collectives: 81.8 us -> 51.3 us  [the longest x1 26.4 us: body(): pieces = lax.all_to_all(plane, 'z', 0, 0, tiled=True)]
    pallas_call x0 -> x2, Pallas kernels: none -> 24.6 us  [the longest x1 23 us: histograms(): pl.pallas_call(functools.partial(hist_kernel, block, together), out_shape...]
    eq x16 -> x0, other arithmetic: 21.1 us -> none  [one_block(): onehot = (columns[:, :, None] == levels[None, None, :]).astype(jnp.bfloat16)]
    all_to_all x0 -> x1, waiting for transfers between devices: none -> 12.1 us  [body(): heard = lax.all_to_all(told, ('x', 'z'), 0, 0, tiled=True)]
    another operation x1 -> x0, loops' own time: 11 us -> none  [build_block(): lax.map(one_block, jnp.arange(count // block_size, dtype=jnp.int32))]
    dynamic_update_slice x16 -> x0, local copies, waits for them, and re-layouts: 10.5 us -> none  [build_block(): lax.map(one_block, jnp.arange(count // block_size, dtype=jnp.int32))]
  transfers between devices with their start and end apart: 0 -> 2, of which waited for: 0 -> 2; matrix products, arithmetic and copies ran while one was open for 0% -> 1% of each run, Pallas kernels for 0% -> 0%
where the time goes in v1:
time: 105 us
  blocking collectives  51.3 us (49%)
  Pallas kernels  24.6 us (23%)
  waiting for transfers between devices  14.7 us (14%)
  starting transfers between devices  7.45 us (7%)
  local copies, waits for them, and re-layouts  3.86 us (4%)
  other arithmetic  2.15 us (2%)
    all_to_all x1, blocking collectives, body(): pieces = lax.all_to_all(plane, 'z', 0, 0, tiled=True)  26.4 us
    all_to_all x1, blocking collectives, body(): plane = jnp.sum(lax.all_to_all(chip, ('y', 'x'), 0, 0, tiled=True), axis=0)  24.9 us
    pallas_call x1, Pallas kernels, histograms(): pl.pallas_call(functools.partial(hist_kernel, block, together), out_shape...  23 us
    all_to_all x1, waiting for transfers between devices, body(): heard = lax.all_to_all(told, ('x', 'z'), 0, 0, tiled=True)  12.1 us
    all_to_all x1, starting transfers between devices, body(): heard = lax.all_to_all(told, ('x', 'z'), 0, 0, tiled=True)  5.53 us
    unnamed x5, local copies, waits for them, and re-layouts  3.61 us
    ppermute x1, waiting for transfers between devices, body(): chip = keep + lax.ppermute(send, 'core', [(0, 1), (1, 0)])  2.63 us
  transfers between devices with their start and end apart: 2, of which 2 were waited for; matrix products, arithmetic and copies ran while one was open for 1% of the time, Pallas kernels for 0%

profile of v1, /device:TPU:2, one launch (start us, length us, event | category | flops | bytes accessed | tf_op | source)
XLA Modules:
  0.0 104.7 jit_solution(9822836989948834693)
XLA Ops:
  0.6 0.7 multiply_add_fusion
  1.3 0.1 reshape.71
  1.4 0.1 broadcast_in_dim.11
  1.5 0.7 bitcast_convert_fusion
  2.2 0.1 broadcast_in_dim.12.target_ref
  2.3 0.0 copy-start
  2.3 1.6 %copy-done = s32[4096,128]{1,0:T(8,128)S(1)} copy-done((s32[4096,128]{1,0:T(8,128)S(1)}, s32[4096,128]{1,0:T(8,128)}, u32[]{:S(2)}) %copy-start) | copy-done | bytes 2097176
  3.9 0.0 copy-start.1
  3.9 0.7 copy-done.1
  4.6 23.0 %histograms.1 = (f32[4,64,8,128]{3,2,1,0:T(8,128)S(1)}, f32[4,64,8,128]{3,2,1,0:T(8,128)S(1)}) custom-call(s32[4096,128]{1,0:T(8,128)S(1)} %copy-done, f32[32,128]{1,0:T(8,128)S(1)} %get-tuple-element.17.grad_ref, f32[32,128]{1,0:T(8,128)S(1)} %get-tuple-element.16.hess_ref, s32[32,128]{1,0:T(8,128)S(1)} %bitcast.14, s32[64,128]{1,0:T(8,128)S(1)} %broadcast_in_dim.12.target_ref), custom_call_target="tpu_custom_call" | custom-call | tf_op jit(solution)/shard_map/histograms/pallas_call | solution.py:72
  27.6 1.9 %collective-permute-start = (f32[4,64,8,128]{3,2,1,0:T(8,128)S(1)}, f32[4,64,8,128]{3,2,1,0:T(8,128)S(1)}, u32[]{:S(2)}, u32[]{:S(2)}) collective-permute-start(f32[4,64,8,128]{3,2,1,0:T(8,128)S(1)} %get-tuple-element.7), channel_id=1, source_target_pairs={{0,64},{64,0},{1,65},{65,1},{2,66},{66,2},{3,67},{67,3},{4,68},{68... | collective-permute-start | bytes 3145736 | tf_op jit(solution)/shard_map/ppermute | solution.py:144
  29.5 2.6 %collective-permute-done = f32[4,64,8,128]{3,2,1,0:T(8,128)S(1)} collective-permute-done((f32[4,64,8,128]{3,2,1,0:T(8,128)S(1)}, f32[4,64,8,128]{3,2,1,0:T(8,128)S(1)}, u32[]{:S(2)}, u32[]{:S(2)}) %collective-permute-start) | collective-permute-done | bytes 1048608 | tf_op jit(solution)/shard_map/ppermute | solution.py:144
  32.2 0.1 add.7
  32.3 24.9 %all_to_all.19 = f32[16,16,8,128]{3,2,1,0:T(8,128)S(1)} all-to-all(f32[16,16,8,128]{3,2,1,0:T(8,128)S(1)} %bitcast.15), channel_id=1, replica_groups=mesh['y'=4,'core'=2,'x'=4,'z'=16] {'y','x'}, dimensions={0} | all-to-all | bytes 2097152 | tf_op jit(solution)/shard_map/all_to_all | solution.py:146
  57.1 0.1 reduce_sum.9
  57.2 26.4 %all_to_all.20.pieces_ref = f32[16,8,128]{2,1,0:T(8,128)} all-to-all(f32[16,8,128]{2,1,0:T(8,128)S(1)} %reduce_sum.9), channel_id=1, replica_groups=mesh['y'=4,'core'=2,'x'=4,'z'=16] {'z'}, dimensions={0} | all-to-all | bytes 131072 | tf_op jit(solution)/shard_map/all_to_all | solution.py:147
  83.6 1.6 %gains.1 = (f32[4,2]{1,0:T(4,128)}, f32[64,128]{1,0:T(8,128)}) custom-call(f32[16,8,128]{2,1,0:T(8,128)} %all_to_all.20.pieces_ref), custom_call_target="tpu_custom_call" | custom-call | tf_op jit(solution)/shard_map/gains/pallas_call | solution.py:111
  85.2 5.5 %all-to-all-start.2 = ((f32[64,1,128]{2,1,0:T(1,128)}), f32[64,1,128]{2,1,0:T(1,128)S(1)}, u32[]{:S(2)}, u32[]{:S(2)}) async-start(f32[64,1,128]{2,1,0:T(1,128)} %bitcast.16), calls=%async_computation.2 | async-start | bytes 65536 | tf_op jit(solution)/shard_map/all_to_all | solution.py:149
  90.7 1.3 %copy.9 = f32[4,2]{0,1:T(2,128)} copy(f32[4,2]{1,0:T(4,128)} %get-tuple-element.12) | data formatting | bytes 64
  92.0 12.1 %all-to-all-done.2 = f32[64,1,128]{2,1,0:T(1,128)S(1)} async-done(((f32[64,1,128]{2,1,0:T(1,128)}), f32[64,1,128]{2,1,0:T(1,128)S(1)}, u32[]{:S(2)}, u32[]{:S(2)}) %all-to-all-start.2) | async-done | bytes 32800 | tf_op jit(solution)/shard_map/all_to_all | solution.py:149
  104.1 0.6 reduce_max.9
  (3 shorter events, 0.0 us)
Async XLA Ops:
  2.3 1.6 %copy-start = (s32[4096,128]{1,0:T(8,128)S(1)}, s32[4096,128]{1,0:T(8,128)}, u32[]{:S(2)}) copy-start(s32[4096,128]{1,0:T(8,128)} %bin_ref.1) | copy-start | bytes 6291460
  3.9 0.7 copy-start.1
  27.6 4.6 %collective-permute-start = (f32[4,64,8,128]{3,2,1,0:T(8,128)S(1)}, f32[4,64,8,128]{3,2,1,0:T(8,128)S(1)}, u32[]{:S(2)}, u32[]{:S(2)}) collective-permute-start(f32[4,64,8,128]{3,2,1,0:T(8,128)S(1)} %get-tuple-element.7), channel_id=1, source_target_pairs={{0,64},{64,0},{1,65},{65,1},{2,66},{66,2},{3,67},{67,3},{4,68},{68... | collective-permute-start | bytes 3145736 | tf_op jit(solution)/shard_map/ppermute | solution.py:144
  85.2 18.9 %all-to-all-start.2 = ((f32[64,1,128]{2,1,0:T(1,128)}), f32[64,1,128]{2,1,0:T(1,128)S(1)}, u32[]{:S(2)}, u32[]{:S(2)}) async-start(f32[64,1,128]{2,1,0:T(1,128)} %bitcast.16), calls=%async_computation.2 | async-start | bytes 65536 | tf_op jit(solution)/shard_map/all_to_all | solution.py:149

commit v2 on v1

v2 whole, which is shorter than its diff:
```python
import functools

import jax
import jax.numpy as jnp
from jax import lax
from jax.experimental import pallas as pl
from jax.experimental.pallas import tpu as pltpu
from jax.sharding import Mesh
from jax.sharding import PartitionSpec as P

BINS = 64
LANES = 128
AXES = ("y", "core", "x", "z")
reg_lambda = 1.0


def hist_kernel(block, together, side_hbm, bin_ref, grad_hbm, hess_hbm, child_hbm,
                keep_ref, send_ref, side_ref, grad_ref, hess_ref, child_ref, arrived, packed, copied):
    rows, features = bin_ref.shape
    leaves = side_ref.shape[0]
    blocks = rows // block
    wide = block // LANES
    bins = pltpu.make_async_copy(bin_ref, arrived, copied.at[4])
    small = [
        pltpu.make_async_copy(source, target, copied.at[i])
        for i, (source, target) in enumerate(
            [(side_hbm, side_ref), (child_hbm, child_ref), (grad_hbm, grad_ref), (hess_hbm, hess_ref)]
        )
    ]
    for copy in small + [bins]:
        copy.start()
    keep_ref[...] = jnp.zeros_like(keep_ref)
    send_ref[...] = jnp.zeros_like(send_ref)

    for copy in small:
        copy.wait()
    mine = lax.axis_index("core")
    child = child_ref[...]
    code = jnp.zeros(child.shape, jnp.int32)
    for leaf in range(leaves):
        y, core, low = leaf // 8, leaf // 4 % 2, leaf % 4
        place = (core ^ mine) * (leaves // 2) + y * 4 + low
        code = jnp.where(child == 2 * leaf + side_ref[leaf], place + 1, code)
    code = code.astype(jnp.float32)
    member = jnp.where(code > 0.0, 1.0, 0.0)

    lane = [lax.broadcasted_iota(jnp.int32, (LANES, LANES), d) for d in (0, 1)]
    before = jnp.where(lane[0] < lane[1], 1.0, 0.0).astype(jnp.bfloat16)
    lines = child.shape[0]
    line = [lax.broadcasted_iota(jnp.int32, (lines, lines), d) for d in (0, 1)]
    above = jnp.where(line[1] < line[0], 1.0, 0.0).astype(jnp.bfloat16)
    short = member.astype(jnp.bfloat16)
    rank = jnp.dot(short, before, preferred_element_type=jnp.float32)
    count = jnp.dot(short, jnp.ones((LANES, LANES), jnp.bfloat16), preferred_element_type=jnp.float32)
    base = jnp.dot(above, count.astype(jnp.bfloat16), preferred_element_type=jnp.float32)
    dest = jnp.where(code > 0.0, rank + base, -2.0 * rows)
    grad = grad_ref[...].astype(jnp.float32)
    hess = hess_ref[...].astype(jnp.float32)

    level = lax.broadcasted_iota(jnp.int32, (16, block), 0).astype(jnp.float32)
    slots = [(level + 16.0 * n).astype(jnp.bfloat16) for n in range(block // 16)]
    one = jnp.ones((16, block), jnp.bfloat16)
    zero = jnp.zeros((16, block), jnp.bfloat16)

    def wide_row(array, s):
        return jnp.concatenate([array[i : i + 1, :] for i in range(s * wide, (s + 1) * wide)], axis=1)

    fill = jnp.zeros((13, block), jnp.float32)
    counts = [jnp.sum(member[s * wide : (s + 1) * wide, :]).astype(jnp.int32) for s in range(blocks)]
    done = [jnp.int32(0)]
    for n in counts:
        done.append(done[-1] + n)
    current = jnp.zeros((features + 16, block), jnp.float32)
    bins.wait()
    for s in range(blocks):
        first, last = (lax.div(n, block) for n in done[s : s + 2])
        values = jnp.concatenate(
            [
                arrived[s * block : (s + 1) * block, :].astype(jnp.float32).T,
                wide_row(code, s), wide_row(grad, s), wide_row(hess, s), fill,
            ],
            axis=0,
        ).astype(jnp.bfloat16)
        slot = wide_row(dest, s) - (first * block).astype(jnp.float32)
        moved = []
        for half in range(2):
            near = jnp.broadcast_to(slot - float(half * block), (16, block)).astype(jnp.bfloat16)
            moved += [jnp.where(near == n, one, zero) for n in slots]
        placed = lax.dot_general(
            values, jnp.concatenate(moved, axis=0), (((1,), (1,)), ((), ())),
            preferred_element_type=jnp.float32,
        )
        current = current + placed[:, :block]
        packed[first] = current
        current = jnp.where(last > first, placed[:, block:], current)
    packed[lax.div(done[-1], block)] = current

    sub = lax.broadcasted_iota(jnp.int32, (8, block), 0)
    is_grad = sub < 4
    place = (sub % 4 + 1).astype(jnp.float32)
    levels = slots[: BINS // 16]

    def one_block(k, carry):
        value = jnp.where(is_grad, packed[k, features + 1 : features + 2, :], packed[k, features + 2 : features + 3, :])
        owned = packed[k, features : features + 1, :] - place
        weights = jnp.concatenate(
            [jnp.where(owned == float(4 * n), value, 0.0) for n in range(leaves // 4)], axis=0
        ).astype(jnp.bfloat16)
        for group in range(features // together):
            upto = []
            for f in range(group * together, (group + 1) * together):
                row = jnp.broadcast_to(packed[k, f : f + 1, :], (16, block)).astype(jnp.bfloat16)
                upto += [jnp.where(row <= n, one, zero) for n in levels]
            part = lax.dot_general(
                weights, jnp.concatenate(upto, axis=0), (((1,), (1,)), ((), ())),
                preferred_element_type=jnp.float32,
            )
            for pair in range(together * BINS // LANES):
                owner = group * (together * BINS // LANES) + pair
                for n in range(leaves // 4):
                    out = keep_ref if n < leaves // 8 else send_ref
                    out[n % (leaves // 8), owner] += part[8 * n : 8 * n + 8, pair * LANES : (pair + 1) * LANES]
        return carry

    lax.fori_loop(0, lax.div(done[-1] + (block - 1), block), one_block, 0)


def histograms(bin_index, gradient, hessian, child_id, smaller_side, block=256, together=4):
    rows, features = bin_index.shape
    leaves = smaller_side.shape[0]
    lines = (rows // LANES, LANES)
    half = jax.ShapeDtypeStruct((leaves // 8, features * BINS // LANES, 8, LANES), jnp.float32)
    vmem = pl.BlockSpec(memory_space=pltpu.VMEM)
    return pl.pallas_call(
        functools.partial(hist_kernel, block, together),
        out_shape=(half, half),
        in_specs=[pl.BlockSpec(memory_space=pltpu.HBM)] * 5,
        out_specs=(vmem, vmem),
        scratch_shapes=[
            pltpu.SMEM((leaves,), jnp.int32),
            pltpu.VMEM(lines, jnp.bfloat16),
            pltpu.VMEM(lines, jnp.bfloat16),
            pltpu.VMEM(lines, jnp.int32),
            pltpu.VMEM((rows, features), jnp.int32),
            pltpu.VMEM((rows // block + 1, features + 16, block), jnp.float32),
            pltpu.SemaphoreType.DMA((5,)),
        ],
        compiler_params=pltpu.CompilerParams(vmem_limit_bytes=60 * 2**20),
        name="histograms",
    )(smaller_side, bin_index, gradient.reshape(lines), hessian.reshape(lines), child_id.reshape(lines))


def gain_kernel(pieces_ref, best_ref, told_ref):
    left = jnp.sum(pieces_ref[...], axis=0)
    lane = lax.broadcasted_iota(jnp.int32, (8, LANES), 1)
    first = jnp.sum(jnp.where(lane == BINS - 1, left, 0.0), axis=1, keepdims=True)
    second = jnp.sum(jnp.where(lane == 2 * BINS - 1, left, 0.0), axis=1, keepdims=True)
    total = jnp.where(lane < BINS, first, second)
    left_grad, left_hess = left[:4], left[4:]
    total_grad, total_hess = total[:4], total[4:]
    right_grad = total_grad - left_grad
    value = left_grad * left_grad / (left_hess + reg_lambda)
    value = value + right_grad * right_grad / (total_hess - left_hess + reg_lambda)
    value = value - total_grad * total_grad / (total_hess + reg_lambda)
    lane = lane[:4]
    bottom = jnp.float32(-jnp.inf)
    inner = lane % BINS < BINS - 1
    one = jnp.max(jnp.where(inner & (lane < BINS), value, bottom), axis=1, keepdims=True)
    two = jnp.max(jnp.where(inner & (lane >= BINS), value, bottom), axis=1, keepdims=True)
    best_ref[...] = jnp.concatenate([one, two], axis=1)
    diagonal = lane == lax.broadcasted_iota(jnp.int32, (4, LANES), 0)
    told = jnp.sum(jnp.where(diagonal, jnp.maximum(one, two), 0.0), axis=0, keepdims=True)
    told_ref[...] = jnp.broadcast_to(told, told_ref.shape)


def gains(pieces, listeners):
    vmem = pl.BlockSpec(memory_space=pltpu.VMEM)
    return pl.pallas_call(
        gain_kernel,
        out_shape=(
            jax.ShapeDtypeStruct((4, 2), jnp.float32),
            jax.ShapeDtypeStruct((listeners, LANES), jnp.float32),
        ),
        in_specs=[vmem],
        out_specs=(vmem, vmem),
        compiler_params=pltpu.CompilerParams(vmem_limit_bytes=4 * 2**20),
        name="gains",
    )(pieces)


def body(bin_index, gradient, hessian, child_id, smaller_side):
    ny, nc, nx, nz = (lax.axis_size(a) for a in AXES)
    keep, send = histograms(bin_index, gradient, hessian, child_id, smaller_side)
    chip = keep + lax.ppermute(send, "core", [(0, 1), (1, 0)])
    chip = chip.reshape(ny * nx, nz, 8, LANES)
    plane = jnp.sum(lax.all_to_all(chip, ("y", "x"), 0, 0, tiled=True), axis=0)
    pieces = lax.all_to_all(plane, "z", 0, 0, tiled=True)
    best_gain, told = gains(pieces, nx * nz)
    heard = lax.all_to_all(told, ("x", "z"), 0, 0, tiled=True)
    child_best = jnp.max(heard, axis=0)[:4]
    return best_gain, child_best


def solution(mesh):
    split = Mesh(mesh.devices.reshape(4, 2, 4, 16), AXES)
    every = P(AXES)
    return jax.shard_map(
        body,
        mesh=split,
        in_specs=(P(AXES, None), every, every, every, P()),
        out_specs=(P(("y", "core"), ("x", "z")), P(("y", "core"))),
        check_vma=False,
    )
```

time: 105 us -> 95.9 us (0.913)
  Pallas kernels: 24.6 us -> 17.9 us
  local copies, waits for them, and re-layouts: 3.86 us -> 0.65 us
    pallas_call x1, Pallas kernels: 23 us -> 17.1 us  [histograms(): pl.pallas_call(functools.partial(hist_kernel, block, together), out_shape...]
    unnamed x5 -> x1, local copies, waits for them, and re-layouts: 3.61 us -> 0.65 us
    add x1, other arithmetic: 0.11 us -> 1.33 us  [body(): chip = keep + lax.ppermute(send, 'core', [(0, 1), (1, 0)])]
where the time goes in v2:
time: 95.9 us; the launch traced here: 95.5 us
  blocking collectives  51.1 us (53%)
  Pallas kernels  17.9 us (19%)
  waiting for transfers between devices  15.7 us (16%)
  starting transfers between devices  7.53 us (8%)
  other arithmetic  1.98 us (2%)
    all_to_all x1, blocking collectives, body(): pieces = lax.all_to_all(plane, 'z', 0, 0, tiled=True)  26.3 us
    all_to_all x1, blocking collectives, body(): plane = jnp.sum(lax.all_to_all(chip, ('y', 'x'), 0, 0, tiled=True), axis=0)  24.8 us
    pallas_call x1, Pallas kernels, histograms(): pl.pallas_call(functools.partial(hist_kernel, block, together), out_shape...  17.1 us
    all_to_all x1, waiting for transfers between devices, body(): heard = lax.all_to_all(told, ('x', 'z'), 0, 0, tiled=True)  12.9 us
    all_to_all x1, starting transfers between devices, body(): heard = lax.all_to_all(told, ('x', 'z'), 0, 0, tiled=True)  5.61 us
    ppermute x1, waiting for transfers between devices, body(): chip = keep + lax.ppermute(send, 'core', [(0, 1), (1, 0)])  2.84 us
    ppermute x1, starting transfers between devices, body(): chip = keep + lax.ppermute(send, 'core', [(0, 1), (1, 0)])  1.92 us
  transfers between devices with their start and end apart: 2, of which 2 were waited for; matrix products, arithmetic and copies ran while one was open for 1% of the time, Pallas kernels for 0%

profile of v2, /device:TPU:2, one launch (start us, length us, event | category | flops | bytes accessed | tf_op | source)
XLA Modules:
  0.0 95.5 jit_solution(1750575525689597884)
XLA Ops:
  0.6 17.1 %histograms.1 = (f32[4,64,8,128]{3,2,1,0:T(8,128)}, f32[4,64,8,128]{3,2,1,0:T(8,128)}) custom-call(s32[32]{0:T(128)} %side_hbm.1, s32[4096,128]{1,0:T(8,128)} %bin_ref.1, bf16[32,128]{1,0:T(8,128)(2,1)} %bitcast.10, bf16[32,128]{1,0:T(8,128)(2,1)} %bitcast.11, s32[32,128]{1,0:T(8,128)} %bitcast.9), custom_call_target="tpu_custom_call" | custom-call | tf_op jit(solution)/shard_map/histograms/pallas_call | solution.py:134
  17.7 1.9 %collective-permute-start = (f32[4,64,8,128]{3,2,1,0:T(8,128)}, f32[4,64,8,128]{3,2,1,0:T(8,128)S(1)}, u32[]{:S(2)}, u32[]{:S(2)}) collective-permute-start(f32[4,64,8,128]{3,2,1,0:T(8,128)} %get-tuple-element.7), channel_id=1, source_target_pairs={{0,64},{64,0},{1,65},{65,1},{2,66},{66,2},{3,67},{67,3},{4,68},{68... | collective-permute-start | bytes 3145736 | tf_op jit(solution)/shard_map/ppermute | solution.py:194
  19.6 2.8 %collective-permute-done = f32[4,64,8,128]{3,2,1,0:T(8,128)S(1)} collective-permute-done((f32[4,64,8,128]{3,2,1,0:T(8,128)}, f32[4,64,8,128]{3,2,1,0:T(8,128)S(1)}, u32[]{:S(2)}, u32[]{:S(2)}) %collective-permute-start) | collective-permute-done | bytes 1048608 | tf_op jit(solution)/shard_map/ppermute | solution.py:194
  22.5 1.3 %add.3 = f32[4,64,8,128]{3,2,1,0:T(8,128)S(1)} add(f32[4,64,8,128]{3,2,1,0:T(8,128)} %get-tuple-element.6, f32[4,64,8,128]{3,2,1,0:T(8,128)S(1)} %collective-permute-done) | non-fusion elementwise | flops 262144 | bytes 3145728 | tf_op jit(solution)/shard_map/add | solution.py:194
  23.8 24.8 %all_to_all.19 = f32[16,16,8,128]{3,2,1,0:T(8,128)S(1)} all-to-all(f32[16,16,8,128]{3,2,1,0:T(8,128)S(1)} %bitcast.8), channel_id=1, replica_groups=mesh['y'=4,'core'=2,'x'=4,'z'=16] {'y','x'}, dimensions={0} | all-to-all | bytes 2097152 | tf_op jit(solution)/shard_map/all_to_all | solution.py:196
  48.6 0.1 reduce_sum.9
  48.7 26.3 %all_to_all.20.pieces_ref = f32[16,8,128]{2,1,0:T(8,128)S(1)} all-to-all(f32[16,8,128]{2,1,0:T(8,128)S(1)} %reduce_sum.9), channel_id=1, replica_groups=mesh['y'=4,'core'=2,'x'=4,'z'=16] {'z'}, dimensions={0} | all-to-all | bytes 131072 | tf_op jit(solution)/shard_map/all_to_all | solution.py:197
  75.0 0.8 gains.1
  75.8 5.6 %all-to-all-start.2 = ((f32[64,1,128]{2,1,0:T(1,128)}), f32[64,1,128]{2,1,0:T(1,128)S(1)}, u32[]{:S(2)}, u32[]{:S(2)}) async-start(f32[64,1,128]{2,1,0:T(1,128)} %bitcast.5), calls=%async_computation.2 | async-start | bytes 65536 | tf_op jit(solution)/shard_map/all_to_all | solution.py:199
  81.4 0.6 copy.9
  82.1 12.9 %all-to-all-done.2 = f32[64,1,128]{2,1,0:T(1,128)S(1)} async-done(((f32[64,1,128]{2,1,0:T(1,128)}), f32[64,1,128]{2,1,0:T(1,128)S(1)}, u32[]{:S(2)}, u32[]{:S(2)}) %all-to-all-start.2) | async-done | bytes 32800 | tf_op jit(solution)/shard_map/all_to_all | solution.py:199
  94.9 0.6 reduce_max.9
Async XLA Ops:
  17.7 4.8 %collective-permute-start = (f32[4,64,8,128]{3,2,1,0:T(8,128)}, f32[4,64,8,128]{3,2,1,0:T(8,128)S(1)}, u32[]{:S(2)}, u32[]{:S(2)}) collective-permute-start(f32[4,64,8,128]{3,2,1,0:T(8,128)} %get-tuple-element.7), channel_id=1, source_target_pairs={{0,64},{64,0},{1,65},{65,1},{2,66},{66,2},{3,67},{67,3},{4,68},{68... | collective-permute-start | bytes 3145736 | tf_op jit(solution)/shard_map/ppermute | solution.py:194
  75.8 19.1 %all-to-all-start.2 = ((f32[64,1,128]{2,1,0:T(1,128)}), f32[64,1,128]{2,1,0:T(1,128)S(1)}, u32[]{:S(2)}, u32[]{:S(2)}) async-start(f32[64,1,128]{2,1,0:T(1,128)} %bitcast.5), calls=%async_computation.2 | async-start | bytes 65536 | tf_op jit(solution)/shard_map/all_to_all | solution.py:199

commit v3 on v2

--- a/solution.py
+++ b/solution.py
@@ -14,7 +14,7 @@
 reg_lambda = 1.0
 
 
-def hist_kernel(block, together, side_hbm, bin_ref, grad_hbm, hess_hbm, child_hbm,
+def hist_kernel(block, joined, together, side_hbm, bin_ref, grad_hbm, hess_hbm, child_hbm,
                 keep_ref, send_ref, side_ref, grad_ref, hess_ref, child_ref, arrived, packed, copied):
     rows, features = bin_ref.shape
     leaves = side_ref.shape[0]
@@ -95,21 +95,31 @@
         current = jnp.where(last > first, placed[:, block:], current)
     packed[lax.div(done[-1], block)] = current
 
-    sub = lax.broadcasted_iota(jnp.int32, (8, block), 0)
+    for n in range(1, joined):
+        packed[lax.div(done[-1], block) + n] = jnp.zeros((features + 16, block), jnp.float32)
+
+    span = joined * block
+    sub = lax.broadcasted_iota(jnp.int32, (8, span), 0)
     is_grad = sub < 4
     place = (sub % 4 + 1).astype(jnp.float32)
-    levels = slots[: BINS // 16]
-
-    def one_block(k, carry):
-        value = jnp.where(is_grad, packed[k, features + 1 : features + 2, :], packed[k, features + 2 : features + 3, :])
-        owned = packed[k, features : features + 1, :] - place
+    level = lax.broadcasted_iota(jnp.int32, (16, span), 0).astype(jnp.float32)
+    levels = [(level + 16.0 * n).astype(jnp.bfloat16) for n in range(BINS // 16)]
+    one = jnp.ones((16, span), jnp.bfloat16)
+    zero = jnp.zeros((16, span), jnp.bfloat16)
+
+    def some_blocks(k, carry):
+        def line(i):
+            return jnp.concatenate([packed[k * joined + n, i : i + 1, :] for n in range(joined)], axis=1)
+
+        value = jnp.where(is_grad, line(features + 1), line(features + 2))
+        owned = line(features) - place
         weights = jnp.concatenate(
             [jnp.where(owned == float(4 * n), value, 0.0) for n in range(leaves // 4)], axis=0
         ).astype(jnp.bfloat16)
         for group in range(features // together):
             upto = []
             for f in range(group * together, (group + 1) * together):
-                row = jnp.broadcast_to(packed[k, f : f + 1, :], (16, block)).astype(jnp.bfloat16)
+                row = jnp.broadcast_to(line(f), (16, span)).astype(jnp.bfloat16)
                 upto += [jnp.where(row <= n, one, zero) for n in levels]
             part = lax.dot_general(
                 weights, jnp.concatenate(upto, axis=0), (((1,), (1,)), ((), ())),
@@ -122,17 +132,17 @@
                     out[n % (leaves // 8), owner] += part[8 * n : 8 * n + 8, pair * LANES : (pair + 1) * LANES]
         return carry
 
-    lax.fori_loop(0, lax.div(done[-1] + (block - 1), block), one_block, 0)
-
-
-def histograms(bin_index, gradient, hessian, child_id, smaller_side, block=256, together=4):
+    lax.fori_loop(0, lax.div(done[-1] + (span - 1), span), some_blocks, 0)
+
+
+def histograms(bin_index, gradient, hessian, child_id, smaller_side, block=256, joined=3, together=4):
     rows, features = bin_index.shape
     leaves = smaller_side.shape[0]
     lines = (rows // LANES, LANES)
-    half = jax.ShapeDtypeStruct((leaves // 8, features * BINS // LANES, 8, LANES), jnp.float32)
+    half = pltpu.VMEM((leaves // 8, features * BINS // LANES, 8, LANES), jnp.float32)
     vmem = pl.BlockSpec(memory_space=pltpu.VMEM)
     return pl.pallas_call(
-        functools.partial(hist_kernel, block, together),
+        functools.partial(hist_kernel, block, joined, together),
         out_shape=(half, half),
         in_specs=[pl.BlockSpec(memory_space=pltpu.HBM)] * 5,
         out_specs=(vmem, vmem),
@@ -142,12 +152,20 @@
             pltpu.VMEM(lines, jnp.bfloat16),
             pltpu.VMEM(lines, jnp.int32),
             pltpu.VMEM((rows, features), jnp.int32),
-            pltpu.VMEM((rows // block + 1, features + 16, block), jnp.float32),
+            pltpu.VMEM((rows // block + joined, features + 16, block), jnp.float32),
             pltpu.SemaphoreType.DMA((5,)),
         ],
-        compiler_params=pltpu.CompilerParams(vmem_limit_bytes=60 * 2**20),
+        compiler_params=pltpu.CompilerParams(vmem_limit_bytes=40 * 2**20),
         name="histograms",
-    )(smaller_side, bin_index, gradient.reshape(lines), hessian.reshape(lines), child_id.reshape(lines))
+    )(
+        *(
+            pltpu.with_memory_space_constraint(a, pltpu.HBM)
+            for a in (
+                smaller_side, bin_index,
+                gradient.reshape(lines), hessian.reshape(lines), child_id.reshape(lines),
+            )
+        )
+    )
 
 
 def gain_kernel(pieces_ref, best_ref, told_ref):

time: 95.9 us -> 92.3 us (0.962)
  Pallas kernels: 17.9 us -> 15.8 us
  other arithmetic: 1.98 us -> 0.76 us
    pallas_call x1, Pallas kernels: 17.1 us -> 15 us  [histograms(): pl.pallas_call(functools.partial(hist_kernel, block, joined, together), o...]
    add x1, other arithmetic: 1.33 us -> 0.11 us  [body(): chip = keep + lax.ppermute(send, 'core', [(0, 1), (1, 0)])]
where the time goes in v3:
time: 92.3 us; the launch traced here: 92 us
  blocking collectives  51.1 us (55%)
  Pallas kernels  15.8 us (17%)
  waiting for transfers between devices  15.5 us (17%)
  starting transfers between devices  7.53 us (8%)
    all_to_all x1, blocking collectives, body(): pieces = lax.all_to_all(plane, 'z', 0, 0, tiled=True)  26.3 us
    all_to_all x1, blocking collectives, body(): plane = jnp.sum(lax.all_to_all(chip, ('y', 'x'), 0, 0, tiled=True), axis=0)  24.9 us
    pallas_call x1, Pallas kernels, histograms(): pl.pallas_call(functools.partial(hist_kernel, block, joined, together), o...  15 us
    all_to_all x1, waiting for transfers between devices, body(): heard = lax.all_to_all(told, ('x', 'z'), 0, 0, tiled=True)  12.9 us
    all_to_all x1, starting transfers between devices, body(): heard = lax.all_to_all(told, ('x', 'z'), 0, 0, tiled=True)  5.61 us
    ppermute x1, waiting for transfers between devices, body(): chip = keep + lax.ppermute(send, 'core', [(0, 1), (1, 0)])  2.63 us
    ppermute x1, starting transfers between devices, body(): chip = keep + lax.ppermute(send, 'core', [(0, 1), (1, 0)])  1.92 us
  transfers between devices with their start and end apart: 2, of which 2 were waited for; matrix products, arithmetic and copies ran while one was open for 1% of the time, Pallas kernels for 0%

profile of v3, /device:TPU:2, one launch (start us, length us, event | category | flops | bytes accessed | tf_op | source)
XLA Modules:
  0.0 92.0 jit_solution(12645432461430347436)
XLA Ops:
  0.6 15.0 %histograms.1 = (f32[4,64,8,128]{3,2,1,0:T(8,128)S(1)}, f32[4,64,8,128]{3,2,1,0:T(8,128)S(1)}) custom-call(s32[32]{0:T(128)} %side_hbm.1, s32[4096,128]{1,0:T(8,128)} %bin_ref.1, bf16[32,128]{1,0:T(8,128)(2,1)} %bitcast.10, bf16[32,128]{1,0:T(8,128)(2,1)} %bitcast.11, s32[32,128]{1,0:T(8,128)} %bitcast.9), custom_call_target="tpu_custom_call" | custom-call | tf_op jit(solution)/shard_map/histograms/pallas_call | solution.py:144
  15.6 1.9 %collective-permute-start = (f32[4,64,8,128]{3,2,1,0:T(8,128)S(1)}, f32[4,64,8,128]{3,2,1,0:T(8,128)S(1)}, u32[]{:S(2)}, u32[]{:S(2)}) collective-permute-start(f32[4,64,8,128]{3,2,1,0:T(8,128)S(1)} %get-tuple-element.7), channel_id=1, source_target_pairs={{0,64},{64,0},{1,65},{65,1},{2,66},{66,2},{3,67},{67,3},{4,68},{68... | collective-permute-start | bytes 3145736 | tf_op jit(solution)/shard_map/ppermute | solution.py:212
  17.6 2.6 %collective-permute-done = f32[4,64,8,128]{3,2,1,0:T(8,128)S(1)} collective-permute-done((f32[4,64,8,128]{3,2,1,0:T(8,128)S(1)}, f32[4,64,8,128]{3,2,1,0:T(8,128)S(1)}, u32[]{:S(2)}, u32[]{:S(2)}) %collective-permute-start) | collective-permute-done | bytes 1048608 | tf_op jit(solution)/shard_map/ppermute | solution.py:212
  20.2 0.1 add.3
  20.3 24.9 %all_to_all.19 = f32[16,16,8,128]{3,2,1,0:T(8,128)S(1)} all-to-all(f32[16,16,8,128]{3,2,1,0:T(8,128)S(1)} %bitcast.8), channel_id=1, replica_groups=mesh['y'=4,'core'=2,'x'=4,'z'=16] {'y','x'}, dimensions={0} | all-to-all | bytes 2097152 | tf_op jit(solution)/shard_map/all_to_all | solution.py:214
  45.1 0.1 reduce_sum.9
  45.2 26.3 %all_to_all.20.pieces_ref = f32[16,8,128]{2,1,0:T(8,128)S(1)} all-to-all(f32[16,8,128]{2,1,0:T(8,128)S(1)} %reduce_sum.9), channel_id=1, replica_groups=mesh['y'=4,'core'=2,'x'=4,'z'=16] {'z'}, dimensions={0} | all-to-all | bytes 131072 | tf_op jit(solution)/shard_map/all_to_all | solution.py:215
  71.5 0.8 gains.1
  72.3 5.6 %all-to-all-start.2 = ((f32[64,1,128]{2,1,0:T(1,128)}), f32[64,1,128]{2,1,0:T(1,128)S(1)}, u32[]{:S(2)}, u32[]{:S(2)}) async-start(f32[64,1,128]{2,1,0:T(1,128)} %bitcast.5), calls=%async_computation.2 | async-start | bytes 65536 | tf_op jit(solution)/shard_map/all_to_all | solution.py:217
  77.9 0.6 copy.9
  78.6 12.9 %all-to-all-done.2 = f32[64,1,128]{2,1,0:T(1,128)S(1)} async-done(((f32[64,1,128]{2,1,0:T(1,128)}), f32[64,1,128]{2,1,0:T(1,128)S(1)}, u32[]{:S(2)}, u32[]{:S(2)}) %all-to-all-start.2) | async-done | bytes 32800 | tf_op jit(solution)/shard_map/all_to_all | solution.py:217
  91.4 0.6 reduce_max.9
Async XLA Ops:
  15.6 4.6 %collective-permute-start = (f32[4,64,8,128]{3,2,1,0:T(8,128)S(1)}, f32[4,64,8,128]{3,2,1,0:T(8,128)S(1)}, u32[]{:S(2)}, u32[]{:S(2)}) collective-permute-start(f32[4,64,8,128]{3,2,1,0:T(8,128)S(1)} %get-tuple-element.7), channel_id=1, source_target_pairs={{0,64},{64,0},{1,65},{65,1},{2,66},{66,2},{3,67},{67,3},{4,68},{68... | collective-permute-start | bytes 3145736 | tf_op jit(solution)/shard_map/ppermute | solution.py:212
  72.3 19.1 %all-to-all-start.2 = ((f32[64,1,128]{2,1,0:T(1,128)}), f32[64,1,128]{2,1,0:T(1,128)S(1)}, u32[]{:S(2)}, u32[]{:S(2)}) async-start(f32[64,1,128]{2,1,0:T(1,128)} %bitcast.5), calls=%async_computation.2 | async-start | bytes 65536 | tf_op jit(solution)/shard_map/all_to_all | solution.py:217

commit v4 on v3

--- a/solution.py
+++ b/solution.py
@@ -10,8 +10,14 @@
 
 BINS = 64
 LANES = 128
-AXES = ("y", "core", "x", "z")
+AXES = ("y", "core", "x", "zh", "zm", "zp")
+Z_PARTS = (4, 2, 2)
 reg_lambda = 1.0
+
+
+def position(owner):
+    x, zh, zm, zp = owner // 16, owner // 4 % 4, owner // 2 % 2, owner % 2
+    return x * 16 + zp * 8 + zm * 4 + zh
 
 
 def hist_kernel(block, joined, together, side_hbm, bin_ref, grad_hbm, hess_hbm, child_hbm,
@@ -129,7 +135,7 @@
                 owner = group * (together * BINS // LANES) + pair
                 for n in range(leaves // 4):
                     out = keep_ref if n < leaves // 8 else send_ref
-                    out[n % (leaves // 8), owner] += part[8 * n : 8 * n + 8, pair * LANES : (pair + 1) * LANES]
+                    out[n % (leaves // 8), position(owner)] += part[8 * n : 8 * n + 8, pair * LANES : (pair + 1) * LANES]
         return carry
 
     lax.fori_loop(0, lax.div(done[-1] + (span - 1), span), some_blocks, 0)
@@ -169,7 +175,23 @@
 
 
 def gain_kernel(pieces_ref, best_ref, told_ref):
+    tiles = pieces_ref.shape[1]
+    mine = lax.axis_index("zh")
     left = jnp.sum(pieces_ref[...], axis=0)
+    best = [tile_gains(left[t]) for t in range(tiles)]
+    one, two = best[0]
+    highest = jnp.maximum(one, two)
+    for t in range(1, tiles):
+        one = jnp.where(mine == t, best[t][0], one)
+        two = jnp.where(mine == t, best[t][1], two)
+        highest = jnp.maximum(highest, jnp.maximum(*best[t]))
+    best_ref[...] = jnp.concatenate([one, two], axis=1)
+    lane, leaf = (lax.broadcasted_iota(jnp.int32, (4, LANES), d) for d in (1, 0))
+    told = jnp.sum(jnp.where(lane == leaf, highest, 0.0), axis=0, keepdims=True)
+    told_ref[...] = jnp.broadcast_to(told, told_ref.shape)
+
+
+def tile_gains(left):
     lane = lax.broadcasted_iota(jnp.int32, (8, LANES), 1)
     first = jnp.sum(jnp.where(lane == BINS - 1, left, 0.0), axis=1, keepdims=True)
     second = jnp.sum(jnp.where(lane == 2 * BINS - 1, left, 0.0), axis=1, keepdims=True)
@@ -185,10 +207,7 @@
     inner = lane % BINS < BINS - 1
     one = jnp.max(jnp.where(inner & (lane < BINS), value, bottom), axis=1, keepdims=True)
     two = jnp.max(jnp.where(inner & (lane >= BINS), value, bottom), axis=1, keepdims=True)
-    best_ref[...] = jnp.concatenate([one, two], axis=1)
-    diagonal = lane == lax.broadcasted_iota(jnp.int32, (4, LANES), 0)
-    told = jnp.sum(jnp.where(diagonal, jnp.maximum(one, two), 0.0), axis=0, keepdims=True)
-    told_ref[...] = jnp.broadcast_to(told, told_ref.shape)
+    return one, two
 
 
 def gains(pieces, listeners):
@@ -207,25 +226,26 @@
 
 
 def body(bin_index, gradient, hessian, child_id, smaller_side):
-    ny, nc, nx, nz = (lax.axis_size(a) for a in AXES)
+    ny, nc, nx, nh, nm, np_ = (lax.axis_size(a) for a in AXES)
     keep, send = histograms(bin_index, gradient, hessian, child_id, smaller_side)
     chip = keep + lax.ppermute(send, "core", [(0, 1), (1, 0)])
-    chip = chip.reshape(ny * nx, nz, 8, LANES)
-    plane = jnp.sum(lax.all_to_all(chip, ("y", "x"), 0, 0, tiled=True), axis=0)
-    pieces = lax.all_to_all(plane, "z", 0, 0, tiled=True)
-    best_gain, told = gains(pieces, nx * nz)
-    heard = lax.all_to_all(told, ("x", "z"), 0, 0, tiled=True)
+    chip = chip.reshape(ny * nx * np_, nm * nh, 8, LANES)
+    near = jnp.sum(lax.all_to_all(chip, ("y", "x", "zp"), 0, 0, tiled=True), axis=0)
+    near = jnp.broadcast_to(near.reshape(nm, 1, nh, 8, LANES), (nm, nh, nh, 8, LANES))
+    pieces = lax.all_to_all(near.reshape(nm * nh, nh, 8, LANES), ("zm", "zh"), 0, 0, tiled=True)
+    best_gain, told = gains(pieces, nx * nm * np_)
+    heard = lax.all_to_all(told, ("x", "zm", "zp"), 0, 0, tiled=True)
     child_best = jnp.max(heard, axis=0)[:4]
     return best_gain, child_best
 
 
 def solution(mesh):
-    split = Mesh(mesh.devices.reshape(4, 2, 4, 16), AXES)
+    split = Mesh(mesh.devices.reshape(4, 2, 4, *Z_PARTS), AXES)
     every = P(AXES)
     return jax.shard_map(
         body,
         mesh=split,
         in_specs=(P(AXES, None), every, every, every, P()),
-        out_specs=(P(("y", "core"), ("x", "z")), P(("y", "core"))),
+        out_specs=(P(("y", "core"), ("x", "zh", "zm", "zp")), P(("y", "core"))),
         check_vma=False,
     )

time: 92.3 us -> 87.6 us (0.949)
  the two profiles are of different devices: /device:TPU:2 before, /device:TPU:8 now
where the time goes in v4:
time: 87.6 us; the launch traced here: 87.3 us
  blocking collectives  51.8 us (59%)
  Pallas kernels  16.1 us (18%)
  waiting for transfers between devices  9.85 us (11%)
  starting transfers between devices  7.55 us (9%)
    all_to_all x1, blocking collectives, body(): lax.all_to_all(near.reshape(nm * nh, nh, 8, LANES), ('zm', 'zh'), 0, 0, t...  27.4 us
    all_to_all x1, blocking collectives, body(): lax.all_to_all(chip, ('y', 'x', 'zp'), 0, 0, tiled=True)  24.4 us
    pallas_call x1, Pallas kernels, histograms(): pl.pallas_call(functools.partial(hist_kernel, block, joined, together), o...  15.3 us
    all_to_all x1, waiting for transfers between devices, body(): heard = lax.all_to_all(told, ('x', 'zm', 'zp'), 0, 0, tiled=True)  7.23 us
    all_to_all x1, starting transfers between devices, body(): heard = lax.all_to_all(told, ('x', 'zm', 'zp'), 0, 0, tiled=True)  5.63 us
    ppermute x1, waiting for transfers between devices, body(): chip = keep + lax.ppermute(send, 'core', [(0, 1), (1, 0)])  2.63 us
    ppermute x1, starting transfers between devices, body(): chip = keep + lax.ppermute(send, 'core', [(0, 1), (1, 0)])  1.92 us
  transfers between devices with their start and end apart: 2, of which 2 were waited for; matrix products, arithmetic and copies ran while one was open for 1% of the time, Pallas kernels for 0%

profile of v4, /device:TPU:8, one launch (start us, length us, event | category | flops | bytes accessed | tf_op | source)
XLA Modules:
  0.0 87.3 jit_solution(8692128690123862264)
XLA Ops:
  0.6 15.3 %histograms.1 = (f32[4,64,8,128]{3,2,1,0:T(8,128)S(1)}, f32[4,64,8,128]{3,2,1,0:T(8,128)S(1)}) custom-call(s32[32]{0:T(128)} %side_hbm.1, s32[4096,128]{1,0:T(8,128)} %bin_ref.1, bf16[32,128]{1,0:T(8,128)(2,1)} %bitcast.14, bf16[32,128]{1,0:T(8,128)(2,1)} %bitcast.15, s32[32,128]{1,0:T(8,128)} %bitcast.13), custom_call_target="tpu_custom_call" | custom-call | tf_op jit(solution)/shard_map/histograms/pallas_call | solution.py:150
  15.9 1.9 %collective-permute-start = (f32[4,64,8,128]{3,2,1,0:T(8,128)S(1)}, f32[4,64,8,128]{3,2,1,0:T(8,128)S(1)}, u32[]{:S(2)}, u32[]{:S(2)}) collective-permute-start(f32[4,64,8,128]{3,2,1,0:T(8,128)S(1)} %get-tuple-element.7), channel_id=1, source_target_pairs={{0,64},{64,0},{1,65},{65,1},{2,66},{66,2},{3,67},{67,3},{4,68},{68... | collective-permute-start | bytes 3145736 | tf_op jit(solution)/shard_map/ppermute | solution.py:231
  17.9 2.6 %collective-permute-done = f32[4,64,8,128]{3,2,1,0:T(8,128)S(1)} collective-permute-done((f32[4,64,8,128]{3,2,1,0:T(8,128)S(1)}, f32[4,64,8,128]{3,2,1,0:T(8,128)S(1)}, u32[]{:S(2)}, u32[]{:S(2)}) %collective-permute-start) | collective-permute-done | bytes 1048608 | tf_op jit(solution)/shard_map/ppermute | solution.py:231
  20.5 0.1 add.3
  20.6 24.4 %all_to_all.19 = f32[32,8,8,128]{3,2,1,0:T(8,128)S(1)} all-to-all(f32[32,8,8,128]{3,2,1,0:T(8,128)S(1)} %bitcast.10), channel_id=1, replica_groups=mesh['y'=4,'core'=2,'x'=4,'zh'=4,'zm'=2,'zp'=2] {'y','x','zp'}, dimensions={0} | all-to-all | bytes 2097152 | tf_op jit(solution)/shard_map/all_to_all | solution.py:233
  45.0 0.1 reduce_sum.9
  45.1 27.4 %all_to_all.20.pieces_ref = f32[8,4,8,128]{3,2,1,0:T(8,128)S(1)} all-to-all(f32[8,4,8,128]{3,2,1,0:T(8,128)S(1)} %bitcast.11), channel_id=1, replica_groups=mesh['y'=4,'core'=2,'x'=4,'zh'=4,'zm'=2,'zp'=2] {'zm','zh'}, dimensions={0} | all-to-all | bytes 262144 | tf_op jit(solution)/shard_map/all_to_all | solution.py:235
  72.5 0.8 gains.1
  73.3 5.6 %all-to-all-start.2 = ((f32[16,1,128]{2,1,0:T(1,128)}), f32[16,1,128]{2,1,0:T(1,128)S(1)}, u32[]{:S(2)}, u32[]{:S(2)}) async-start(f32[16,1,128]{2,1,0:T(1,128)} %bitcast.7), calls=%async_computation.2 | async-start | bytes 16384 | tf_op jit(solution)/shard_map/all_to_all | solution.py:237
  78.9 0.6 copy.9
  79.6 7.2 %all-to-all-done.2 = f32[16,1,128]{2,1,0:T(1,128)S(1)} async-done(((f32[16,1,128]{2,1,0:T(1,128)}), f32[16,1,128]{2,1,0:T(1,128)S(1)}, u32[]{:S(2)}, u32[]{:S(2)}) %all-to-all-start.2) | async-done | bytes 8224 | tf_op jit(solution)/shard_map/all_to_all | solution.py:237
  86.8 0.5 reduce_max.9
  (1 shorter events, 0.0 us)
Async XLA Ops:
  15.9 4.6 %collective-permute-start = (f32[4,64,8,128]{3,2,1,0:T(8,128)S(1)}, f32[4,64,8,128]{3,2,1,0:T(8,128)S(1)}, u32[]{:S(2)}, u32[]{:S(2)}) collective-permute-start(f32[4,64,8,128]{3,2,1,0:T(8,128)S(1)} %get-tuple-element.7), channel_id=1, source_target_pairs={{0,64},{64,0},{1,65},{65,1},{2,66},{66,2},{3,67},{67,3},{4,68},{68... | collective-permute-start | bytes 3145736 | tf_op jit(solution)/shard_map/ppermute | solution.py:231
  73.3 13.5 %all-to-all-start.2 = ((f32[16,1,128]{2,1,0:T(1,128)}), f32[16,1,128]{2,1,0:T(1,128)S(1)}, u32[]{:S(2)}, u32[]{:S(2)}) async-start(f32[16,1,128]{2,1,0:T(1,128)} %bitcast.7), calls=%async_computation.2 | async-start | bytes 16384 | tf_op jit(solution)/shard_map/all_to_all | solution.py:237

commit v5 on v4

--- a/solution.py
+++ b/solution.py
@@ -21,7 +21,7 @@
 
 
 def hist_kernel(block, joined, together, side_hbm, bin_ref, grad_hbm, hess_hbm, child_hbm,
-                keep_ref, send_ref, side_ref, grad_ref, hess_ref, child_ref, arrived, packed, copied):
+                keep_ref, send_ref, side_ref, grad_ref, hess_ref, child_ref, arrived, packed, odd_sums, copied):
     rows, features = bin_ref.shape
     leaves = side_ref.shape[0]
     blocks = rows // block
@@ -35,8 +35,8 @@
     ]
     for copy in small + [bins]:
         copy.start()
-    keep_ref[...] = jnp.zeros_like(keep_ref)
-    send_ref[...] = jnp.zeros_like(send_ref)
+    for ref in (keep_ref, send_ref, odd_sums):
+        ref[...] = jnp.zeros_like(ref)
 
     for copy in small:
         copy.wait()
@@ -104,41 +104,54 @@
     for n in range(1, joined):
         packed[lax.div(done[-1], block) + n] = jnp.zeros((features + 16, block), jnp.float32)
 
-    span = joined * block
-    sub = lax.broadcasted_iota(jnp.int32, (8, span), 0)
+    sub = lax.broadcasted_iota(jnp.int32, (8, block), 0)
     is_grad = sub < 4
     place = (sub % 4 + 1).astype(jnp.float32)
-    level = lax.broadcasted_iota(jnp.int32, (16, span), 0).astype(jnp.float32)
-    levels = [(level + 16.0 * n).astype(jnp.bfloat16) for n in range(BINS // 16)]
-    one = jnp.ones((16, span), jnp.bfloat16)
-    zero = jnp.zeros((16, span), jnp.bfloat16)
-
-    def some_blocks(k, carry):
-        def line(i):
-            return jnp.concatenate([packed[k * joined + n, i : i + 1, :] for n in range(joined)], axis=1)
-
-        value = jnp.where(is_grad, line(features + 1), line(features + 2))
-        owned = line(features) - place
-        weights = jnp.concatenate(
-            [jnp.where(owned == float(4 * n), value, 0.0) for n in range(leaves // 4)], axis=0
-        ).astype(jnp.bfloat16)
-        for group in range(features // together):
-            upto = []
-            for f in range(group * together, (group + 1) * together):
-                row = jnp.broadcast_to(line(f), (16, span)).astype(jnp.bfloat16)
-                upto += [jnp.where(row <= n, one, zero) for n in levels]
-            part = lax.dot_general(
-                weights, jnp.concatenate(upto, axis=0), (((1,), (1,)), ((), ())),
-                preferred_element_type=jnp.float32,
+    levels = slots[: BINS // 16]
+    groups = features // together
+    tiles = together * BINS // LANES
+    contract = (((1,), (1,)), ((), ()))
+
+    def out_tile(owner, n):
+        return (keep_ref if n < leaves // 8 else send_ref).at[n % (leaves // 8), position(owner)]
+
+    def some_blocks(step, carry):
+        for k in (step * joined + n for n in range(joined)):
+            value = jnp.where(
+                is_grad,
+                packed[k, features + 1 : features + 2, :],
+                packed[k, features + 2 : features + 3, :],
             )
-            for pair in range(together * BINS // LANES):
-                owner = group * (together * BINS // LANES) + pair
-                for n in range(leaves // 4):
-                    out = keep_ref if n < leaves // 8 else send_ref
-                    out[n % (leaves // 8), position(owner)] += part[8 * n : 8 * n + 8, pair * LANES : (pair + 1) * LANES]
+            owned = packed[k, features : features + 1, :] - place
+            weights = jnp.concatenate(
+                [jnp.where(owned == float(4 * n), value, 0.0) for n in range(leaves // 4)], axis=0
+            ).astype(jnp.bfloat16)
+            for group in range(groups):
+                upto = []
+                for f in range(group * together, (group + 1) * together):
+                    row = jnp.broadcast_to(packed[k, f : f + 1, :], (16, block)).astype(jnp.bfloat16)
+                    upto += [jnp.where(row <= n, one, zero) for n in levels]
+                upto = jnp.concatenate(upto, axis=0)
+                if group % 2:
+                    odd_sums[group // 2] += lax.dot_general(
+                        upto, weights, contract, preferred_element_type=jnp.float32
+                    )
+                    continue
+                part = lax.dot_general(weights, upto, contract, preferred_element_type=jnp.float32)
+                for tile in range(tiles):
+                    for n in range(leaves // 4):
+                        out = out_tile(group * tiles + tile, n)
+                        out[...] += part[8 * n : 8 * n + 8, tile * LANES : (tile + 1) * LANES]
         return carry
 
+    span = joined * block
     lax.fori_loop(0, lax.div(done[-1] + (span - 1), span), some_blocks, 0)
+    for group in range(1, groups, 2):
+        for tile in range(tiles):
+            part = odd_sums[group // 2, tile * LANES : (tile + 1) * LANES, :].T
+            for n in range(leaves // 4):
+                out = out_tile(group * tiles + tile, n)
+                out[...] = part[8 * n : 8 * n + 8, :]
 
 
 def histograms(bin_index, gradient, hessian, child_id, smaller_side, block=256, joined=3, together=4):
@@ -159,6 +172,7 @@
             pltpu.VMEM(lines, jnp.int32),
             pltpu.VMEM((rows, features), jnp.int32),
             pltpu.VMEM((rows // block + joined, features + 16, block), jnp.float32),
+            pltpu.VMEM((features // together // 2, together * BINS, 2 * leaves), jnp.float32),
             pltpu.SemaphoreType.DMA((5,)),
         ],
         compiler_params=pltpu.CompilerParams(vmem_limit_bytes=40 * 2**20),

time: 87.6 us -> 82.8 us (0.945)
  Pallas kernels: 16.1 us -> 11.3 us
    pallas_call x1, Pallas kernels: 15.3 us -> 10.5 us  [histograms(): pl.pallas_call(functools.partial(hist_kernel, block, joined, together), o...]
where the time goes in v5:
time: 82.8 us; the launch traced here: 82.5 us
  blocking collectives  51.8 us (63%)
  Pallas kernels  11.3 us (14%)
  waiting for transfers between devices  9.85 us (12%)
  starting transfers between devices  7.55 us (9%)
    all_to_all x1, blocking collectives, body(): lax.all_to_all(near.reshape(nm * nh, nh, 8, LANES), ('zm', 'zh'), 0, 0, t...  27.4 us
    all_to_all x1, blocking collectives, body(): lax.all_to_all(chip, ('y', 'x', 'zp'), 0, 0, tiled=True)  24.4 us
    pallas_call x1, Pallas kernels, histograms(): pl.pallas_call(functools.partial(hist_kernel, block, joined, together), o...  10.5 us
    all_to_all x1, waiting for transfers between devices, body(): heard = lax.all_to_all(told, ('x', 'zm', 'zp'), 0, 0, tiled=True)  7.23 us
    all_to_all x1, starting transfers between devices, body(): heard = lax.all_to_all(told, ('x', 'zm', 'zp'), 0, 0, tiled=True)  5.63 us
    ppermute x1, waiting for transfers between devices, body(): chip = keep + lax.ppermute(send, 'core', [(0, 1), (1, 0)])  2.63 us
    ppermute x1, starting transfers between devices, body(): chip = keep + lax.ppermute(send, 'core', [(0, 1), (1, 0)])  1.92 us
  transfers between devices with their start and end apart: 2, of which 2 were waited for; matrix products, arithmetic and copies ran while one was open for 1% of the time, Pallas kernels for 0%

profile of v5, /device:TPU:8, one launch (start us, length us, event | category | flops | bytes accessed | tf_op | source)
XLA Modules:
  0.0 82.5 jit_solution(16893833740769688159)
XLA Ops:
  0.6 10.5 %histograms.1 = (f32[4,64,8,128]{3,2,1,0:T(8,128)S(1)}, f32[4,64,8,128]{3,2,1,0:T(8,128)S(1)}) custom-call(s32[32]{0:T(128)} %side_hbm.1, s32[4096,128]{1,0:T(8,128)} %bin_ref.1, bf16[32,128]{1,0:T(8,128)(2,1)} %bitcast.14, bf16[32,128]{1,0:T(8,128)(2,1)} %bitcast.15, s32[32,128]{1,0:T(8,128)} %bitcast.13), custom_call_target="tpu_custom_call" | custom-call | tf_op jit(solution)/shard_map/histograms/pallas_call | solution.py:163
  11.1 1.9 %collective-permute-start = (f32[4,64,8,128]{3,2,1,0:T(8,128)S(1)}, f32[4,64,8,128]{3,2,1,0:T(8,128)S(1)}, u32[]{:S(2)}, u32[]{:S(2)}) collective-permute-start(f32[4,64,8,128]{3,2,1,0:T(8,128)S(1)} %get-tuple-element.7), channel_id=1, source_target_pairs={{0,64},{64,0},{1,65},{65,1},{2,66},{66,2},{3,67},{67,3},{4,68},{68... | collective-permute-start | bytes 3145736 | tf_op jit(solution)/shard_map/ppermute | solution.py:245
  13.1 2.6 %collective-permute-done = f32[4,64,8,128]{3,2,1,0:T(8,128)S(1)} collective-permute-done((f32[4,64,8,128]{3,2,1,0:T(8,128)S(1)}, f32[4,64,8,128]{3,2,1,0:T(8,128)S(1)}, u32[]{:S(2)}, u32[]{:S(2)}) %collective-permute-start) | collective-permute-done | bytes 1048608 | tf_op jit(solution)/shard_map/ppermute | solution.py:245
  15.7 0.1 add.3
  15.8 24.4 %all_to_all.19 = f32[32,8,8,128]{3,2,1,0:T(8,128)S(1)} all-to-all(f32[32,8,8,128]{3,2,1,0:T(8,128)S(1)} %bitcast.10), channel_id=1, replica_groups=mesh['y'=4,'core'=2,'x'=4,'zh'=4,'zm'=2,'zp'=2] {'y','x','zp'}, dimensions={0} | all-to-all | bytes 2097152 | tf_op jit(solution)/shard_map/all_to_all | solution.py:247
  40.2 0.1 reduce_sum.9
  40.3 27.4 %all_to_all.20.pieces_ref = f32[8,4,8,128]{3,2,1,0:T(8,128)S(1)} all-to-all(f32[8,4,8,128]{3,2,1,0:T(8,128)S(1)} %bitcast.11), channel_id=1, replica_groups=mesh['y'=4,'core'=2,'x'=4,'zh'=4,'zm'=2,'zp'=2] {'zm','zh'}, dimensions={0} | all-to-all | bytes 262144 | tf_op jit(solution)/shard_map/all_to_all | solution.py:249
  67.7 0.8 gains.1
  68.5 5.6 %all-to-all-start.2 = ((f32[16,1,128]{2,1,0:T(1,128)}), f32[16,1,128]{2,1,0:T(1,128)S(1)}, u32[]{:S(2)}, u32[]{:S(2)}) async-start(f32[16,1,128]{2,1,0:T(1,128)} %bitcast.7), calls=%async_computation.2 | async-start | bytes 16384 | tf_op jit(solution)/shard_map/all_to_all | solution.py:251
  74.1 0.6 copy.9
  74.8 7.2 %all-to-all-done.2 = f32[16,1,128]{2,1,0:T(1,128)S(1)} async-done(((f32[16,1,128]{2,1,0:T(1,128)}), f32[16,1,128]{2,1,0:T(1,128)S(1)}, u32[]{:S(2)}, u32[]{:S(2)}) %all-to-all-start.2) | async-done | bytes 8224 | tf_op jit(solution)/shard_map/all_to_all | solution.py:251
  82.0 0.5 reduce_max.9
  (1 shorter events, 0.0 us)
Async XLA Ops:
  11.1 4.6 %collective-permute-start = (f32[4,64,8,128]{3,2,1,0:T(8,128)S(1)}, f32[4,64,8,128]{3,2,1,0:T(8,128)S(1)}, u32[]{:S(2)}, u32[]{:S(2)}) collective-permute-start(f32[4,64,8,128]{3,2,1,0:T(8,128)S(1)} %get-tuple-element.7), channel_id=1, source_target_pairs={{0,64},{64,0},{1,65},{65,1},{2,66},{66,2},{3,67},{67,3},{4,68},{68... | collective-permute-start | bytes 3145736 | tf_op jit(solution)/shard_map/ppermute | solution.py:245
  68.5 13.5 %all-to-all-start.2 = ((f32[16,1,128]{2,1,0:T(1,128)}), f32[16,1,128]{2,1,0:T(1,128)S(1)}, u32[]{:S(2)}, u32[]{:S(2)}) async-start(f32[16,1,128]{2,1,0:T(1,128)} %bitcast.7), calls=%async_computation.2 | async-start | bytes 16384 | tf_op jit(solution)/shard_map/all_to_all | solution.py:251

commit v6 on v5

--- a/solution.py
+++ b/solution.py
@@ -35,8 +35,12 @@
     ]
     for copy in small + [bins]:
         copy.start()
-    for ref in (keep_ref, send_ref, odd_sums):
-        ref[...] = jnp.zeros_like(ref)
+    odd_sums[...] = jnp.zeros_like(odd_sums)
+    tiles = together * BINS // LANES
+    for owner in range(features * BINS // LANES):
+        if owner // tiles % 2 == 0:
+            for ref in (keep_ref, send_ref):
+                ref[:, position(owner)] = jnp.zeros((leaves // 8, 8, LANES), jnp.float32)
 
     for copy in small:
         copy.wait()
@@ -109,7 +113,6 @@
     place = (sub % 4 + 1).astype(jnp.float32)
     levels = slots[: BINS // 16]
     groups = features // together
-    tiles = together * BINS // LANES
     contract = (((1,), (1,)), ((), ()))
 
     def out_tile(owner, n):

time: 82.8 us -> 82.8 us (level)
  the two profiles are of different devices: /device:TPU:8 before, /device:TPU:2 now
where the time goes in v6:
time: 82.8 us; the launch traced here: 82.4 us
  blocking collectives  52.5 us (63%)
  Pallas kernels  11.3 us (14%)
  waiting for transfers between devices  8.49 us (10%)
  starting transfers between devices  8.12 us (10%)
    all_to_all x1, blocking collectives, body(): lax.all_to_all(near.reshape(nm * nh, nh, 8, LANES), ('zm', 'zh'), 0, 0, t...  26.5 us
    all_to_all x1, blocking collectives, body(): lax.all_to_all(chip, ('y', 'x', 'zp'), 0, 0, tiled=True)  25.9 us
    pallas_call x1, Pallas kernels, histograms(): pl.pallas_call(functools.partial(hist_kernel, block, joined, together), o...  10.5 us
    all_to_all x1, starting transfers between devices, body(): heard = lax.all_to_all(told, ('x', 'zm', 'zp'), 0, 0, tiled=True)  6.2 us
    all_to_all x1, waiting for transfers between devices, body(): heard = lax.all_to_all(told, ('x', 'zm', 'zp'), 0, 0, tiled=True)  5.86 us
    ppermute x1, waiting for transfers between devices, body(): chip = keep + lax.ppermute(send, 'core', [(0, 1), (1, 0)])  2.63 us
    ppermute x1, starting transfers between devices, body(): chip = keep + lax.ppermute(send, 'core', [(0, 1), (1, 0)])  1.92 us
  transfers between devices with their start and end apart: 2, of which 2 were waited for; matrix products, arithmetic and copies ran while one was open for 1% of the time, Pallas kernels for 0%

profile of v6, /device:TPU:2, one launch (start us, length us, event | category | flops | bytes accessed | tf_op | source)
XLA Modules:
  0.0 82.4 jit_solution(8645420397817553479)
XLA Ops:
  0.6 10.5 %histograms.1 = (f32[4,64,8,128]{3,2,1,0:T(8,128)S(1)}, f32[4,64,8,128]{3,2,1,0:T(8,128)S(1)}) custom-call(s32[32]{0:T(128)} %side_hbm.1, s32[4096,128]{1,0:T(8,128)} %bin_ref.1, bf16[32,128]{1,0:T(8,128)(2,1)} %bitcast.14, bf16[32,128]{1,0:T(8,128)(2,1)} %bitcast.15, s32[32,128]{1,0:T(8,128)} %bitcast.13), custom_call_target="tpu_custom_call" | custom-call | tf_op jit(solution)/shard_map/histograms/pallas_call | solution.py:166
  11.1 1.9 %collective-permute-start = (f32[4,64,8,128]{3,2,1,0:T(8,128)S(1)}, f32[4,64,8,128]{3,2,1,0:T(8,128)S(1)}, u32[]{:S(2)}, u32[]{:S(2)}) collective-permute-start(f32[4,64,8,128]{3,2,1,0:T(8,128)S(1)} %get-tuple-element.7), channel_id=1, source_target_pairs={{0,64},{64,0},{1,65},{65,1},{2,66},{66,2},{3,67},{67,3},{4,68},{68... | collective-permute-start | bytes 3145736 | tf_op jit(solution)/shard_map/ppermute | solution.py:248
  13.1 2.6 %collective-permute-done = f32[4,64,8,128]{3,2,1,0:T(8,128)S(1)} collective-permute-done((f32[4,64,8,128]{3,2,1,0:T(8,128)S(1)}, f32[4,64,8,128]{3,2,1,0:T(8,128)S(1)}, u32[]{:S(2)}, u32[]{:S(2)}) %collective-permute-start) | collective-permute-done | bytes 1048608 | tf_op jit(solution)/shard_map/ppermute | solution.py:248
  15.7 0.1 add.3
  15.8 25.9 %all_to_all.19 = f32[32,8,8,128]{3,2,1,0:T(8,128)S(1)} all-to-all(f32[32,8,8,128]{3,2,1,0:T(8,128)S(1)} %bitcast.10), channel_id=1, replica_groups=mesh['y'=4,'core'=2,'x'=4,'zh'=4,'zm'=2,'zp'=2] {'y','x','zp'}, dimensions={0} | all-to-all | bytes 2097152 | tf_op jit(solution)/shard_map/all_to_all | solution.py:250
  41.7 0.1 reduce_sum.9
  41.8 26.5 %all_to_all.20.pieces_ref = f32[8,4,8,128]{3,2,1,0:T(8,128)S(1)} all-to-all(f32[8,4,8,128]{3,2,1,0:T(8,128)S(1)} %bitcast.11), channel_id=1, replica_groups=mesh['y'=4,'core'=2,'x'=4,'zh'=4,'zm'=2,'zp'=2] {'zm','zh'}, dimensions={0} | all-to-all | bytes 262144 | tf_op jit(solution)/shard_map/all_to_all | solution.py:252
  68.3 0.8 gains.1
  69.1 6.2 %all-to-all-start.2 = ((f32[16,1,128]{2,1,0:T(1,128)}), f32[16,1,128]{2,1,0:T(1,128)S(1)}, u32[]{:S(2)}, u32[]{:S(2)}) async-start(f32[16,1,128]{2,1,0:T(1,128)} %bitcast.7), calls=%async_computation.2 | async-start | bytes 16384 | tf_op jit(solution)/shard_map/all_to_all | solution.py:254
  75.3 0.6 copy.9
  76.0 5.9 %all-to-all-done.2 = f32[16,1,128]{2,1,0:T(1,128)S(1)} async-done(((f32[16,1,128]{2,1,0:T(1,128)}), f32[16,1,128]{2,1,0:T(1,128)S(1)}, u32[]{:S(2)}, u32[]{:S(2)}) %all-to-all-start.2) | async-done | bytes 8224 | tf_op jit(solution)/shard_map/all_to_all | solution.py:254
  81.8 0.5 reduce_max.9
  (1 shorter events, 0.0 us)
Async XLA Ops:
  11.1 4.6 %collective-permute-start = (f32[4,64,8,128]{3,2,1,0:T(8,128)S(1)}, f32[4,64,8,128]{3,2,1,0:T(8,128)S(1)}, u32[]{:S(2)}, u32[]{:S(2)}) collective-permute-start(f32[4,64,8,128]{3,2,1,0:T(8,128)S(1)} %get-tuple-element.7), channel_id=1, source_target_pairs={{0,64},{64,0},{1,65},{65,1},{2,66},{66,2},{3,67},{67,3},{4,68},{68... | collective-permute-start | bytes 3145736 | tf_op jit(solution)/shard_map/ppermute | solution.py:248
  69.1 12.7 %all-to-all-start.2 = ((f32[16,1,128]{2,1,0:T(1,128)}), f32[16,1,128]{2,1,0:T(1,128)S(1)}, u32[]{:S(2)}, u32[]{:S(2)}) async-start(f32[16,1,128]{2,1,0:T(1,128)} %bitcast.7), calls=%async_computation.2 | async-start | bytes 16384 | tf_op jit(solution)/shard_map/all_to_all | solution.py:254
